TPU v7x, 768 devices: a whole 4x8x12 slice. The times are simulated.
768 devices in a mesh: rep: 48 (over z_lo, y), mp: 16 (over z_hi, x, core).
Axes of the slice: x: 4, y: 8, z: 12 (z_hi: 2, z_lo: 6; z = z_hi * 6 + z_lo), core: 2. Of those that a mesh axis runs over, the one named last changes fastest.
Arguments:
- local_weights: bfloat16 [48, 2, 192, 14336], P('rep', None, None, 'mp'), may hold values from -6 to 6
- base_weights: float32 [2, 192, 14336], P(None, None, 'mp'), may hold values from -6 to 6
- momentum: float32 [2, 192, 14336], P(None, 'rep', 'mp'), may hold values from -4 to 4
- exponents: int32 [48, 2, 192, 112], P('rep', None, None, 'mp'), may hold values from -10 to 0
- mix_ratio: int32 [2], replicated, may hold values from 1 to 16, as said below
Outputs:
- mixed_weights: bfloat16 [48, 2, 192, 14336], P('rep', None, None, 'mp')
- new_base: float32 [2, 192, 14336], P(None, None, 'mp')
- new_momentum: float32 [2, 192, 14336], P(None, 'rep', 'mp')
Inputs may be any that keep to these rules, and one draw needn't show every extreme that they name: mix_ratio[1] is 16 and mix_ratio[0] lies in 1 to 15.
All inputs are finite; a program needn't handle non-finite values.
Results may differ from a plain program's by a relative error of at most 0.012.
Values may be sent and summed in bfloat16 or wider, within the bound.
No kernel may reach another device: no remote copies, remote signals or barrier semaphores. Data moves between devices by JAX's collectives and lax.ppermute only.
A program may use at most 32 MiB of HBM per device.

v0:
```python
import jax
import jax.numpy as jnp
from jax import lax
from jax.sharding import PartitionSpec as P

BLOCK = 128


def shards(local_weights, base_weights, momentum, exponents, mix_ratio):
    replicas = lax.axis_size("rep")
    rows = base_weights.shape[1]
    width = base_weights.shape[2]
    groups = exponents.shape[3]
    owned = rows // replicas
    scales = jnp.exp2(exponents[0].astype(jnp.float32))[..., None]
    delta = (base_weights - local_weights[0].astype(jnp.float32)).reshape(2, rows, groups, BLOCK)
    coded = jnp.clip(delta / scales, -448.0, 448.0).astype(jnp.bfloat16)
    decoded = (coded.astype(jnp.float32) * scales).reshape(2, rows, width)
    summed = lax.psum_scatter(decoded, "rep", scatter_dimension=1, tiled=True)
    average = summed / replicas
    new_momentum = 0.9 * momentum + average
    first_row = lax.axis_index("rep") * owned
    base_owned = lax.dynamic_slice_in_dim(base_weights, first_row, owned, 1)
    base_piece = base_owned - 0.7 * (average + 0.9 * new_momentum)
    new_base = lax.all_gather(base_piece, "rep", axis=1, tiled=True)
    alpha = mix_ratio[0].astype(jnp.float32) / mix_ratio[1].astype(jnp.float32)
    mixed_weights = (
        alpha * local_weights.astype(jnp.float32) + (1.0 - alpha) * new_base[None]
    ).astype(jnp.bfloat16)
    return (mixed_weights, new_base, new_momentum)


def solution(mesh):
    placed = (
        P("rep", None, None, "mp"),
        P(None, None, "mp"),
        P(None, "rep", "mp"),
        P("rep", None, None, "mp"),
        P(),
    )
    return jax.shard_map(
        shards,
        mesh=mesh,
        in_specs=placed,
        out_specs=(P("rep", None, None, "mp"), P(None, None, "mp"), P(None, "rep", "mp")),
        check_vma=False,
    )
```

profile of v0, /device:TPU:2, one launch (start us, length us, event | category | flops | bytes accessed | tf_op | source)
XLA Modules:
  0.0 896.9 jit_solution(9201493764819430821)
XLA Ops:
  7.2 0.0 all-reduce.3.cloned.1.call-start
  7.2 0.7 exponential_bitcast_fusion
  7.9 0.1 copy.10
  8.1 0.5 div.25
  8.6 0.3 div.26
  8.8 2.9 convert_multiply_fusion.1
  11.7 0.0 copy-start.1
  11.7 0.0 copy-start.2
  11.7 0.0 copy-start
  11.7 0.0 all-reduce.3.cloned.1.call-update
  11.7 0.0 all-gather.2.cloned.1.call-start
  11.8 1.3 dynamic-slice
  13.8 584.9 %all-reduce.3.cloned.1.call-done = f32[2,192,896]{2,1,0:T(8,128)} async-done(((f32[2,192,896]{2,1,0:T(8,128)}), f32[2,192,896]{2,1,0:T(8,128)}) %all-reduce.3.cloned.1.call-update) | async-done | bytes 1376272
  598.7 0.0 copy-done.1
  598.7 1.5 multiply_subtract_fusion
  600.2 0.6 copy.11
  600.8 0.0 all-gather.2.cloned.1.call-update
  600.8 0.0 copy-done.2
  600.9 0.6 fusion.6
  602.7 284.6 %all-gather.2.cloned.1.call-done = f32[2,192,896]{2,0,1:T(2,128)} async-done(((f32[2,4,896]{2,0,1:T(2,128)}), f32[2,192,896]{2,0,1:T(2,128)}) %all-gather.2.cloned.1.call-update) | async-done | bytes 1376272 | tf_op jit(solution)/shard_map/all_gather | solution.py:25
  887.3 0.0 copy-done
  887.3 2.8 fusion.1
Async XLA Ops:
  7.2 591.5 %all-reduce.3.cloned.1.call-start = ((), (), s32[]{:S(2)}) async-start(), calls=%async_computation.1 | async-start | bytes 2752512
  11.7 587.0 %copy-start.1 = (f32[2,4,896]{2,1,0:T(4,128)S(1)}, f32[2,4,896]{2,1,0:T(4,128)}, u32[]{:S(2)}) copy-start(f32[2,4,896]{2,1,0:T(4,128)} %param.7) | copy-start | bytes 86020
  11.7 589.1 %copy-start.2 = (s32[2]{0:T(128)S(1)}, s32[2]{0:T(128)}, u32[]{:S(2)}) copy-start(s32[2]{0:T(128)} %param.9) | copy-start | bytes 28
  11.7 875.6 %copy-start = (bf16[1,2,192,896]{3,2,1,0:T(8,128)(2,1)S(1)}, bf16[1,2,192,896]{3,2,1,0:T(8,128)(2,1)}, u32[]{:S(2)}) copy-start(bf16[1,2,192,896]{3,2,1,0:T(8,128)(2,1)} %param.5) | copy-start | bytes 2064388
  11.7 875.6 %all-gather.2.cloned.1.call-start = ((), (), s32[]{:S(2)}) async-start(), calls=%async_computation | async-start | bytes 1404928 | tf_op jit(solution)/shard_map/all_gather | solution.py:25
Sparse Core Ops, SparseCore 0:
  11.9 586.8 all-reduce.2
  602.0 285.2 all-gather.1
where the time goes:
time: 897 us
  waiting for transfers between devices  870 us (97%)
  between operations  16 us (2%)
    unnamed x3, waiting for transfers between devices  585 us
    all_gather x1, waiting for transfers between devices, shards(): new_base = lax.all_gather(base_piece, 'rep', axis=1, tiled=True)  285 us
  transfers between devices with their start and end apart: 2, of which 2 were waited for; matrix products, arithmetic and copies ran while one was open for 0% of the time, Pallas kernels for 0%

commit v1 on v0

v1 whole, which is shorter than its diff:
```python
import functools

import jax
import jax.numpy as jnp
from jax import lax
from jax.experimental import pallas as pl
from jax.experimental.pallas import tpu as pltpu
from jax.sharding import PartitionSpec as P

BLOCK = 128
OUTER = 3
F32 = jnp.float32
BF16 = jnp.bfloat16


def low_rows(shape):
    return lax.broadcasted_iota(jnp.int32, shape, len(shape) - 2) < 4


def encode_kernel(groups, local_ref, base_ref, exp_ref, out_ref):
    width = base_ref.shape[3]
    pieces = [[], [], [], []]
    for outer in range(OUTER):
        halves = []
        for side in range(2):
            delta = base_ref[side, outer] - local_ref[side, outer].astype(F32)
            bound = exp_ref[side, outer]
            bound = jnp.concatenate(
                [jnp.broadcast_to(bound[:, g : g + 1], (16, BLOCK)) for g in range(groups)], axis=1
            )
            coded = jnp.minimum(jnp.maximum(delta, -bound), bound)
            halves.append(coded.reshape(2, 8, width))
        gate, up = halves
        low = low_rows(gate.shape)
        even = jnp.where(low, gate, pltpu.roll(up, 4, 1))
        odd = jnp.where(low, pltpu.roll(gate, 4, 1), up)
        for k in range(2):
            pieces[2 * k].append(even[k])
            pieces[2 * k + 1].append(odd[k])
    for i in range(4):
        out_ref[i] = jnp.concatenate(pieces[i], axis=0).astype(BF16)


def partial_kernel(parts, replicas, outer_ref, got_ref, momentum_ref, send_ref, own_ref):
    mine = outer_ref[0]
    total = got_ref[0].astype(F32)
    for i in range(1, parts):
        total = total + got_ref[i].astype(F32)
    total = total * (1.0 / replicas)
    share = 0.81 * momentum_ref[...]
    own = jnp.zeros_like(share)
    rows = []
    for outer in range(OUTER):
        average = total[8 * outer : 8 * outer + 8]
        here = mine == outer
        own = jnp.where(here, average, own)
        rows.append(1.9 * average + jnp.where(here, share, 0.0))
    own_ref[...] = own
    send = jnp.concatenate(rows, axis=0).astype(BF16)
    for i in range(OUTER):
        send_ref[i] = send


def step_kernel(parts, outer_ref, got_ref, momentum_ref, own_ref, send_ref, new_ref):
    mine = outer_ref[0]
    blocks = [got_ref[i].astype(F32) for i in range(OUTER)]
    total = blocks[0]
    for block in blocks[1:]:
        total = total + block
    send = (0.7 * total).astype(BF16)
    for i in range(parts):
        send_ref[i] = send
    others = jnp.zeros_like(own_ref[...])
    for i in range(OUTER):
        picked = jnp.zeros_like(others)
        for outer in range(OUTER):
            picked = jnp.where(mine == outer, blocks[i][8 * outer : 8 * outer + 8], picked)
        others = others + jnp.where(mine == i, 0.0, picked)
    average = own_ref[...] + others * (1.0 / 1.9)
    new_ref[...] = 0.9 * momentum_ref[...] + average


def mix_kernel(mix_ref, got_ref, local_ref, base_ref, mixed_ref, new_ref):
    width = base_ref.shape[3]
    top = jnp.full((16, width), mix_ref[0].astype(F32))
    bottom = jnp.full((16, width), mix_ref[1].astype(F32))
    alpha = top / bottom
    blocks = [got_ref[i].astype(F32) for i in range(4)]
    for outer in range(OUTER):
        rows = slice(8 * outer, 8 * outer + 8)
        even = jnp.stack([blocks[0][rows], blocks[2][rows]])
        odd = jnp.stack([blocks[1][rows], blocks[3][rows]])
        low = low_rows(even.shape)
        gate = jnp.where(low, even, pltpu.roll(odd, 4, 1)).reshape(16, width)
        up = jnp.where(low, pltpu.roll(even, 4, 1), odd).reshape(16, width)
        for side, update in ((0, gate), (1, up)):
            fresh = base_ref[side, outer] - update
            new_ref[side, outer] = fresh
            kept = local_ref[side, outer].astype(F32)
            mixed_ref[side, outer] = (alpha * kept + (1.0 - alpha) * fresh).astype(BF16)


def shards(local_weights, base_weights, momentum, exponents, mix_ratio):
    replicas = lax.axis_size("rep")
    rows = base_weights.shape[1]
    width = base_weights.shape[2]
    groups = exponents.shape[3]
    parts = replicas // OUTER
    steps = parts // 4
    deep = rows // OUTER
    near = [[o * parts + j for j in range(parts)] for o in range(OUTER)]
    far = [[o * parts + j for o in range(OUTER)] for j in range(parts)]
    outer = (lax.axis_index("rep") // parts).astype(jnp.int32).reshape(1)

    local = local_weights.reshape(2, OUTER, deep, width)
    base = base_weights.reshape(2, OUTER, deep, width)
    bound = (448.0 * jnp.exp2(exponents[0].astype(F32))).reshape(2, OUTER, deep, groups)
    tall = pl.BlockSpec((2, OUTER, 16, width), lambda i: (0, 0, i, 0))
    flat = pl.BlockSpec((4, OUTER * 8, width), lambda i: (i, 0, 0))
    coded = pl.pallas_call(
        functools.partial(encode_kernel, groups),
        grid=(steps,),
        in_specs=[tall, tall, pl.BlockSpec((2, OUTER, 16, groups), lambda i: (0, 0, i, 0))],
        out_specs=flat,
        out_shape=jax.ShapeDtypeStruct((parts, OUTER * 8, width), BF16),
        name="encode",
    )(local, base, bound)
    got = lax.all_to_all(coded, "rep", 0, 0, axis_index_groups=near, tiled=True)
    held = momentum.reshape(8, width)
    scalar = pl.BlockSpec(memory_space=pltpu.SMEM)
    whole = pl.BlockSpec(memory_space=pltpu.VMEM)
    send, own = pl.pallas_call(
        functools.partial(partial_kernel, parts, replicas),
        in_specs=[scalar, whole, whole],
        out_specs=[whole, whole],
        out_shape=[
            jax.ShapeDtypeStruct((OUTER, OUTER * 8, width), BF16),
            jax.ShapeDtypeStruct((8, width), F32),
        ],
        name="partial",
    )(outer, got, held)
    got = lax.all_to_all(send, "rep", 0, 0, axis_index_groups=far, tiled=True)
    send, new_momentum = pl.pallas_call(
        functools.partial(step_kernel, parts),
        in_specs=[scalar, whole, whole, whole],
        out_specs=[whole, whole],
        out_shape=[
            jax.ShapeDtypeStruct((parts, OUTER * 8, width), BF16),
            jax.ShapeDtypeStruct((8, width), F32),
        ],
        name="outer_step",
    )(outer, got, held, own)
    got = lax.all_to_all(send, "rep", 0, 0, axis_index_groups=near, tiled=True)
    mixed, new_base = pl.pallas_call(
        mix_kernel,
        grid=(steps,),
        in_specs=[scalar, flat, tall, tall],
        out_specs=[tall, tall],
        out_shape=[
            jax.ShapeDtypeStruct(local.shape, BF16),
            jax.ShapeDtypeStruct(base.shape, F32),
        ],
        name="mix",
    )(mix_ratio, got, local, base)
    return (
        mixed.reshape(local_weights.shape),
        new_base.reshape(base_weights.shape),
        new_momentum.reshape(momentum.shape),
    )


def solution(mesh):
    placed = (
        P("rep", None, None, "mp"),
        P(None, None, "mp"),
        P(None, "rep", "mp"),
        P("rep", None, None, "mp"),
        P(),
    )
    return jax.shard_map(
        shards,
        mesh=mesh,
        in_specs=placed,
        out_specs=(P("rep", None, None, "mp"), P(None, None, "mp"), P(None, "rep", "mp")),
        check_vma=False,
    )
```

time: 897 us -> 86.6 us (0.10)
  the two profiles are of different devices: /device:TPU:2 before, /device:TPU:12 now
where the time goes in v1:
time: 86.6 us; the launch traced here: 85.9 us
  waiting for transfers between devices  34.8 us (40%)
  blocking collectives  19.8 us (23%)
  starting transfers between devices  14.4 us (17%)
  Pallas kernels  11.7 us (14%)
  local copies, waits for them, and re-layouts  3.77 us (4%)
    all_to_all x1, blocking collectives, shards(): got = lax.all_to_all(send, 'rep', 0, 0, axis_index_groups=far, tiled=True)  19.8 us
    all_to_all x1, waiting for transfers between devices, shards(): got = lax.all_to_all(coded, 'rep', 0, 0, axis_index_groups=near, tiled=True)  18.4 us
    all_to_all x1, waiting for transfers between devices, shards(): got = lax.all_to_all(send, 'rep', 0, 0, axis_index_groups=near, tiled=True)  16.4 us
    all_to_all x1, starting transfers between devices, shards(): got = lax.all_to_all(coded, 'rep', 0, 0, axis_index_groups=near, tiled=True)  9.5 us
    all_to_all x1, starting transfers between devices, shards(): got = lax.all_to_all(send, 'rep', 0, 0, axis_index_groups=near, tiled=True)  4.92 us
    pallas_call x1, Pallas kernels, shards(): pl.pallas_call(mix_kernel, grid=(steps,), in_specs=[scalar, flat, tall, t...  4.11 us
    pallas_call x1, Pallas kernels, shards(): pl.pallas_call(functools.partial(encode_kernel, groups), grid=(steps,), i...  3.91 us
    pallas_call x1, Pallas kernels, shards(): pl.pallas_call(functools.partial(partial_kernel, parts, replicas), in_spe...  1.86 us
  transfers between devices with their start and end apart: 2, of which 2 were waited for; matrix products, arithmetic and copies ran while one was open for 1% of the time, Pallas kernels for 0%

profile of v1, /device:TPU:12, one launch (start us, length us, event | category | flops | bytes accessed | tf_op | source)
XLA Modules:
  0.0 85.9 jit_solution(4111551514036353346)
XLA Ops:
  0.6 0.7 exponential_multiply_fusion
  1.4 0.8 copy.8
  2.2 3.9 %encode.1 = bf16[16,24,896]{2,1,0:T(8,128)(2,1)} custom-call(bf16[2,3,64,896]{3,2,1,0:T(8,128)(2,1)} %bitcast.8, f32[2,3,64,896]{3,2,1,0:T(8,128)} %bitcast.6, f32[2,3,64,7]{3,2,1,0:T(8,128)} %bitcast.10), custom_call_target="tpu_custom_call" | custom-call | tf_op jit(solution)/shard_map/encode/pallas_call | solution.py:120
  6.1 0.0 copy-start.2
  6.1 9.5 %all-to-all-start = ((bf16[16,24,896]{2,1,0:T(8,128)(2,1)}), bf16[16,24,896]{2,1,0:T(8,128)(2,1)S(1)}, u32[]{:S(2)}, u32[]{:S(2)}) async-start(bf16[16,24,896]{2,1,0:T(8,128)(2,1)} %encode.1), calls=%async_computation | async-start | bytes 1376256 | tf_op jit(solution)/shard_map/all_to_all | solution.py:128
  15.6 0.0 copy-done.2
  15.6 0.6 reshape.38.momentum_ref
  16.2 18.4 %all-to-all-done.got_ref = bf16[16,24,896]{2,1,0:T(8,128)(2,1)S(1)} async-done(((bf16[16,24,896]{2,1,0:T(8,128)(2,1)}), bf16[16,24,896]{2,1,0:T(8,128)(2,1)S(1)}, u32[]{:S(2)}, u32[]{:S(2)}) %all-to-all-start) | async-done | bytes 688160 | tf_op jit(solution)/shard_map/all_to_all | solution.py:128
  34.6 0.0 copy-start
  34.6 0.8 copy-done
  35.4 1.9 %partial.1 = (bf16[3,24,896]{2,1,0:T(8,128)(2,1)}, f32[8,896]{1,0:T(8,128)}) custom-call(s32[1]{0:T(128)} %bitcast.outer_ref, bf16[16,24,896]{2,1,0:T(8,128)(2,1)} %copy-done, f32[8,896]{1,0:T(8,128)} %reshape.38.momentum_ref), custom_call_target="tpu_custom_call" | custom-call | tf_op jit(solution)/shard_map/partial/pallas_call | solution.py:132
  37.3 19.8 %all_to_all.15.got_ref = bf16[3,24,896]{2,1,0:T(8,128)(2,1)} all-to-all(bf16[3,24,896]{2,1,0:T(8,128)(2,1)} %get-tuple-element.9), channel_id=1, replica_groups={{0,256,512},{16,272,528},{32,288,544},{48,304,560},{64,320,576},{80,336..., dimensions={0} | all-to-all | bytes 258048 | tf_op jit(solution)/shard_map/all_to_all | solution.py:142
  57.1 1.8 %outer_step.1 = (bf16[16,24,896]{2,1,0:T(8,128)(2,1)}, f32[8,896]{1,0:T(8,128)}) custom-call(s32[1]{0:T(128)} %bitcast.outer_ref, bf16[3,24,896]{2,1,0:T(8,128)(2,1)} %all_to_all.15.got_ref, f32[8,896]{1,0:T(8,128)} %reshape.38.momentum_ref, f32[8,896]{1,0:T(8,128)} %get-tuple-element.10.own_ref), custom_call_target="tpu_custom_call" | custom-call | tf_op jit(solution)/shard_map/outer_step/pallas_call | solution.py:143
  58.9 0.0 copy-start.3
  58.9 4.9 %all-to-all-start.2 = ((bf16[16,24,896]{2,1,0:T(8,128)(2,1)}), bf16[16,24,896]{2,1,0:T(8,128)(2,1)S(1)}, u32[]{:S(2)}, u32[]{:S(2)}) async-start(bf16[16,24,896]{2,1,0:T(8,128)(2,1)} %get-tuple-element.11), calls=%async_computation.2 | async-start | bytes 1376256 | tf_op jit(solution)/shard_map/all_to_all | solution.py:153
  63.9 0.0 copy-done.3
  63.9 0.6 reshape.41
  64.5 16.4 %all-to-all-done.2.got_ref = bf16[16,24,896]{2,1,0:T(8,128)(2,1)S(1)} async-done(((bf16[16,24,896]{2,1,0:T(8,128)(2,1)}), bf16[16,24,896]{2,1,0:T(8,128)(2,1)S(1)}, u32[]{:S(2)}, u32[]{:S(2)}) %all-to-all-start.2) | async-done | bytes 688160 | tf_op jit(solution)/shard_map/all_to_all | solution.py:153
  80.9 0.0 copy-start.1
  80.9 0.8 copy-done.1
  81.8 4.1 %mix.1 = (bf16[2,3,64,896]{3,2,1,0:T(8,128)(2,1)}, f32[2,3,64,896]{3,2,1,0:T(8,128)}) custom-call(s32[2]{0:T(128)} %mix_ref.1, bf16[16,24,896]{2,1,0:T(8,128)(2,1)} %copy-done.1, bf16[2,3,64,896]{3,2,1,0:T(8,128)(2,1)} %bitcast.9, f32[2,3,64,896]{3,2,1,0:T(8,128)} %bitcast.7), custom_call_target="tpu_custom_call" | custom-call | tf_op jit(solution)/shard_map/mix/pallas_call | solution.py:154
Async XLA Ops:
  6.1 9.5 %copy-start.2 = (f32[2,4,896]{2,1,0:T(4,128)S(1)}, f32[2,4,896]{2,1,0:T(4,128)}, u32[]{:S(2)}) copy-start(f32[2,4,896]{2,1,0:T(4,128)} %param.7) | copy-start | bytes 86020
  6.1 28.5 %all-to-all-start = ((bf16[16,24,896]{2,1,0:T(8,128)(2,1)}), bf16[16,24,896]{2,1,0:T(8,128)(2,1)S(1)}, u32[]{:S(2)}, u32[]{:S(2)}) async-start(bf16[16,24,896]{2,1,0:T(8,128)(2,1)} %encode.1), calls=%async_computation | async-start | bytes 1376256 | tf_op jit(solution)/shard_map/all_to_all | solution.py:128
  34.6 0.8 copy-start
  58.9 4.9 %copy-start.3 = (f32[8,896]{1,0:T(8,128)S(1)}, f32[8,896]{1,0:T(8,128)}, u32[]{:S(2)}) copy-start(f32[8,896]{1,0:T(8,128)} %get-tuple-element.14) | copy-start | bytes 86020
  58.9 22.0 %all-to-all-start.2 = ((bf16[16,24,896]{2,1,0:T(8,128)(2,1)}), bf16[16,24,896]{2,1,0:T(8,128)(2,1)S(1)}, u32[]{:S(2)}, u32[]{:S(2)}) async-start(bf16[16,24,896]{2,1,0:T(8,128)(2,1)} %get-tuple-element.11), calls=%async_computation.2 | async-start | bytes 1376256 | tf_op jit(solution)/shard_map/all_to_all | solution.py:153
  80.9 0.8 copy-start.1

commit v2 on v0

v2 whole, which is shorter than its diff:
```python
import functools

import jax
import jax.numpy as jnp
from jax import lax
from jax.experimental import pallas as pl
from jax.experimental.pallas import tpu as pltpu
from jax.sharding import PartitionSpec as P

BLOCK = 128
OUTER = 2
ROUND = 8
TALL = 16
F32 = jnp.float32
BF16 = jnp.bfloat16
SMALL = pltpu.CompilerParams(vmem_limit_bytes=12 << 20)
SCALAR = pl.BlockSpec(memory_space=pltpu.SMEM)
WHOLE = pl.BlockSpec(memory_space=pltpu.VMEM)
FAR = pl.BlockSpec(memory_space=pltpu.HBM)


def slot(member):
    layer = member // ROUND
    return (layer ^ 1 if layer < 2 else layer) * ROUND + member % ROUND


def low_rows(shape):
    return lax.broadcasted_iota(jnp.int32, shape, len(shape) - 2) < 4


def encode_kernel(place_ref, exp_hbm, local_hbm, base_hbm, out_ref, rows_ref, exp_ref, local_ref, base_ref, bound_ref, sems):
    _, _, deep, width = base_ref.shape
    steps = deep // TALL
    load_exp = pltpu.make_async_copy(exp_hbm, exp_ref, sems.at[2 * steps])
    load_exp.start()
    loads = []
    for step in range(steps):
        rows = pl.ds(TALL * step, TALL)
        for k, (source, target) in enumerate(((local_hbm, local_ref), (base_hbm, base_ref))):
            load = pltpu.make_async_copy(source.at[:, :, rows], target.at[:, :, rows], sems.at[2 * step + k])
            load.start()
            loads.append(load)
    load_exp.wait()
    groups = exp_ref.shape[0]
    where = lax.broadcasted_iota(jnp.int32, (groups, width), 1) // BLOCK
    spread = (where == lax.broadcasted_iota(jnp.int32, (groups, width), 0)).astype(BF16)
    for side in range(2):
        power = (1 << (exp_ref[:, side, :] + 10)).astype(F32) * (448.0 / 1024.0)
        bound_ref[side] = lax.dot_general(
            power.astype(BF16), spread, (((0,), (0,)), ((), ())), preferred_element_type=F32
        )
    tiles = TALL // 8
    for step in range(steps):
        rows = pl.ds(TALL * step, TALL)
        loads[2 * step].wait()
        loads[2 * step + 1].wait()
        pieces = [[] for _ in range(2 * tiles)]
        for outer in range(OUTER):
            halves = []
            for side in range(2):
                delta = base_ref[side, outer, rows] - local_ref[side, outer, rows].astype(F32)
                bound = bound_ref[side, pl.ds(outer * deep + TALL * step, TALL)]
                coded = jnp.minimum(jnp.maximum(delta, -bound), bound)
                halves.append(coded.reshape(tiles, 8, width))
            gate, up = halves
            low = low_rows(gate.shape)
            even = jnp.where(low, gate, pltpu.roll(up, 4, 1))
            odd = jnp.where(low, pltpu.roll(gate, 4, 1), up)
            for k in range(tiles):
                pieces[2 * k].append(even[k])
                pieces[2 * k + 1].append(odd[k])
        for i in range(2 * tiles):
            out_ref[slot(2 * tiles * step + i)] = jnp.concatenate(pieces[i], axis=0).astype(BF16)
    odd = place_ref[1] == 1
    mine = pl.ds(pl.multiple_of(place_ref[2] * 8, 8), 8)
    low = low_rows((8, width))
    for outer in range(OUTER):
        gate, up = base_ref[0, outer, mine], base_ref[1, outer, mine]
        first = jnp.where(odd, pltpu.roll(gate, 4, 0), gate)
        second = jnp.where(odd, up, pltpu.roll(up, 4, 0))
        rows_ref[8 * outer : 8 * outer + 8] = jnp.where(low, first, second)


def partial_kernel(parts, replicas, place_ref, got_ref, rows_ref, momentum_ref, send_ref, own_ref, share_ref):
    mine = place_ref[0]
    share_ref[0:4] = 0.567 * momentum_ref[0]
    share_ref[4:8] = 0.567 * momentum_ref[1]
    total = got_ref[0].astype(F32)
    for i in range(1, parts):
        total = total + got_ref[i].astype(F32)
    base = rows_ref[...]
    exact = base * (1.0 / OUTER) - total * (1.33 / replicas)
    share = share_ref[...]
    own = jnp.zeros_like(share)
    sums = []
    for outer in range(OUTER):
        rows = slice(8 * outer, 8 * outer + 8)
        here = mine == outer
        part = exact[rows] - jnp.where(here, share, 0.0)
        rounded = part.astype(BF16)
        own = jnp.where(here, base[rows] - share - (part - rounded.astype(F32)), own)
        sums.append(part)
    own_ref[...] = own
    send_ref[...] = jnp.concatenate(sums, axis=0).astype(BF16)


def step_kernel(parts, place_ref, kept_ref, got_ref, momentum_ref, own_ref, send_ref, new_ref):
    mine = place_ref[0]
    total = kept_ref[...].astype(F32) + got_ref[...].astype(F32)
    send = total.astype(BF16)
    for i in range(parts):
        send_ref[i] = send
    picked = total[0:8]
    for outer in range(1, OUTER):
        picked = jnp.where(mine == outer, total[8 * outer : 8 * outer + 8], picked)
    average = (own_ref[...] - picked) * (1.0 / 1.33)
    for side in range(2):
        new_ref[side] = 0.9 * momentum_ref[side] + average[4 * side : 4 * side + 4]


def mix_kernel(mix_ref, got_ref, local_ref, mixed_hbm, new_hbm, mixed_ref, new_ref, sems):
    _, _, deep, width = new_ref.shape
    tiles = TALL // 8
    top = jnp.full((8, width), mix_ref[0].astype(F32))
    bottom = jnp.full((8, width), mix_ref[1].astype(F32))
    alpha = (top / bottom)[None]
    stores = []
    for step in range(deep // TALL):
        span = pl.ds(TALL * step, TALL)
        blocks = [got_ref[slot(2 * tiles * step + i)].astype(F32) for i in range(2 * tiles)]
        for outer in range(OUTER):
            rows = slice(8 * outer, 8 * outer + 8)
            even = jnp.stack([blocks[2 * k][rows] for k in range(tiles)])
            odd = jnp.stack([blocks[2 * k + 1][rows] for k in range(tiles)])
            low = low_rows(even.shape)
            gate = jnp.where(low, even, pltpu.roll(odd, 4, 1))
            up = jnp.where(low, pltpu.roll(even, 4, 1), odd)
            for side, fresh in ((0, gate), (1, up)):
                new_ref[side, outer, span] = fresh.reshape(TALL, width)
                kept = local_ref[side, outer, span].astype(F32).reshape(tiles, 8, width)
                mixed = alpha * kept + (1.0 - alpha) * fresh
                mixed_ref[side, outer, span] = mixed.reshape(TALL, width).astype(BF16)
        for k, (source, target) in enumerate(((mixed_ref, mixed_hbm), (new_ref, new_hbm))):
            store = pltpu.make_async_copy(source.at[:, :, span], target.at[:, :, span], sems.at[2 * step + k])
            store.start()
            stores.append(store)
    for store in stores:
        store.wait()


def encode(place, exponents, local, base):
    groups, _, rows = exponents.shape
    _, _, deep, width = base.shape
    return pl.pallas_call(
        encode_kernel,
        in_specs=[SCALAR, FAR, FAR, FAR],
        out_specs=[WHOLE, WHOLE],
        out_shape=[
            jax.ShapeDtypeStruct((deep // 4, OUTER * 8, width), BF16),
            jax.ShapeDtypeStruct((OUTER * 8, width), F32),
        ],
        scratch_shapes=[
            pltpu.VMEM(exponents.shape, jnp.int32),
            pltpu.VMEM(local.shape, BF16),
            pltpu.VMEM(base.shape, F32),
            pltpu.VMEM((2, rows, width), F32),
            pltpu.SemaphoreType.DMA((2 * (deep // TALL) + 1,)),
        ],
        compiler_params=SMALL,
        name="encode",
    )(place, *(pltpu.with_memory_space_constraint(x, pltpu.HBM) for x in (exponents, local, base)))


def partial(replicas, place, got, rows, momentum):
    parts, tall, width = got.shape
    return pl.pallas_call(
        functools.partial(partial_kernel, parts, replicas),
        in_specs=[SCALAR, WHOLE, WHOLE, WHOLE],
        out_specs=[WHOLE, WHOLE],
        out_shape=[jax.ShapeDtypeStruct((tall, width), BF16), jax.ShapeDtypeStruct((8, width), F32)],
        scratch_shapes=[pltpu.VMEM((8, width), F32)],
        compiler_params=SMALL,
        name="partial",
    )(place, got, rows, momentum)


def outer_step(parts, place, kept, got, momentum, own):
    tall, width = got.shape
    return pl.pallas_call(
        functools.partial(step_kernel, parts),
        in_specs=[SCALAR, WHOLE, WHOLE, WHOLE, WHOLE],
        out_specs=[WHOLE, WHOLE],
        out_shape=[jax.ShapeDtypeStruct((parts, tall, width), BF16), jax.ShapeDtypeStruct(momentum.shape, F32)],
        compiler_params=SMALL,
        name="outer_step",
    )(place, kept, got, momentum, own)


def mix(mix_ratio, got, local):
    deep = local.shape[2]
    return pl.pallas_call(
        mix_kernel,
        in_specs=[SCALAR, WHOLE, WHOLE],
        out_specs=[FAR, FAR],
        out_shape=[jax.ShapeDtypeStruct(local.shape, BF16), jax.ShapeDtypeStruct(local.shape, F32)],
        scratch_shapes=[
            pltpu.VMEM(local.shape, BF16),
            pltpu.VMEM(local.shape, F32),
            pltpu.SemaphoreType.DMA((2 * (deep // TALL),)),
        ],
        compiler_params=SMALL,
        name="mix",
    )(mix_ratio, got, local)


def shards(local_weights, base_weights, momentum, exponents, mix_ratio):
    replicas = lax.axis_size("rep")
    rows, width = base_weights.shape[1:]
    parts = replicas // OUTER
    members = sorted(range(parts), key=slot)
    near = [[o * parts + j for j in members] for o in range(OUTER)]
    across = [(r, (r + parts) % replicas) for r in range(replicas)]
    index = lax.axis_index("rep")
    member = lax.rem(index, parts)
    place = jnp.stack([lax.div(index, parts), lax.rem(member, 2), lax.div(member, 2)]).astype(jnp.int32)
    swap = functools.partial(
        lax.all_to_all, axis_name="rep", split_axis=0, concat_axis=0, axis_index_groups=near, tiled=True
    )

    local = local_weights.reshape(2, OUTER, rows // OUTER, width)
    base = base_weights.reshape(2, OUTER, rows // OUTER, width)
    coded, own_rows = encode(place, jnp.transpose(exponents[0], (2, 0, 1)), local, base)
    sent, own = partial(replicas, place, swap(coded), own_rows, momentum)
    got = lax.ppermute(sent, "rep", across)
    sent, new_momentum = outer_step(parts, place, sent, got, momentum, own)
    mixed, new_base = mix(mix_ratio, swap(sent), local)
    return mixed.reshape(local_weights.shape), new_base.reshape(base_weights.shape), new_momentum


def solution(mesh):
    placed = (
        P("rep", None, None, "mp"),
        P(None, None, "mp"),
        P(None, "rep", "mp"),
        P("rep", None, None, "mp"),
        P(),
    )
    return jax.shard_map(
        shards,
        mesh=mesh,
        in_specs=placed,
        out_specs=(P("rep", None, None, "mp"), P(None, None, "mp"), P(None, "rep", "mp")),
        check_vma=False,
    )
```

time: 897 us -> 71.2 us (0.08)
  the two profiles are of different devices: /device:TPU:2 before, /device:TPU:198 now
where the time goes in v2:
time: 71.2 us; the launch traced here: 71 us
  blocking collectives  56.4 us (79%)
  Pallas kernels  6.23 us (9%)
  waiting for transfers between devices  5.63 us (8%)
  starting transfers between devices  1.92 us (3%)
    all_to_all x1, blocking collectives, shards(): sent, own = partial(replicas, place, swap(coded), own_rows, momentum)  31.4 us
    all_to_all x1, blocking collectives, shards(): mixed, new_base = mix(mix_ratio, swap(sent), local)  25 us
    ppermute x1, waiting for transfers between devices, shards(): got = lax.ppermute(sent, 'rep', across)  5.63 us
    pallas_call x1, Pallas kernels, encode(): pl.pallas_call(encode_kernel, in_specs=[SCALAR, FAR, FAR, FAR], out_specs...  2.37 us
    pallas_call x1, Pallas kernels, mix(): pl.pallas_call(mix_kernel, in_specs=[SCALAR, WHOLE, WHOLE], out_specs=[FA...  2 us
    ppermute x1, starting transfers between devices, shards(): got = lax.ppermute(sent, 'rep', across)  1.92 us
  transfers between devices with their start and end apart: 1, of which 1 were waited for; matrix products, arithmetic and copies ran while one was open for 0% of the time, Pallas kernels for 0%

profile of v2, /device:TPU:198, one launch (start us, length us, event | category | flops | bytes accessed | tf_op | source)
XLA Modules:
  0.0 71.0 jit_solution(5511068956216482692)
XLA Ops:
  0.7 0.1 pad_add_fusion.place_ref
  0.7 0.0 copy-start.1
  0.7 2.4 %encode.1 = (bf16[24,16,896]{2,1,0:T(8,128)(2,1)S(1)}, f32[16,896]{1,0:T(8,128)S(1)}) custom-call(s32[3]{0:T(128)S(1)} %pad_add_fusion.place_ref, s32[7,2,192]{2,1,0:T(2,128)} %bitcast.13, bf16[2,2,96,896]{3,2,1,0:T(8,128)(2,1)} %bitcast.10, f32[2,2,96,896]{3,2,1,0:T(8,128)} %bitcast.12), custom_call_target="tpu_custom_call" | custom-call | tf_op jit(solution)/shard_map/encode/pallas_call | solution.py:154
  3.1 31.4 %all_to_all.10.got_ref = bf16[24,16,896]{2,1,0:T(8,128)(2,1)S(1)} all-to-all(bf16[24,16,896]{2,1,0:T(8,128)(2,1)S(1)} %get-tuple-element.11), channel_id=1, replica_groups={{128,144,160,176,192,208,224,240,0,16,32,48,64,80,96,112,256,272,288,30..., dimensions={0} | all-to-all | bytes 1376256 | tf_op jit(solution)/shard_map/all_to_all | solution.py:233
  34.5 0.0 copy-start
  34.5 0.0 copy-start.2
  34.5 0.0 copy-done.1
  34.5 0.7 partial.1
  35.2 1.9 %collective-permute-start = (bf16[16,896]{1,0:T(8,128)(2,1)S(1)}, bf16[16,896]{1,0:T(8,128)(2,1)S(1)}, u32[]{:S(2)}, u32[]{:S(2)}) collective-permute-start(bf16[16,896]{1,0:T(8,128)(2,1)S(1)} %get-tuple-element.13.kept_ref), channel_id=1, source_target_pairs={{0,384},{16,400},{32,416},{48,432},{64,448},{80,464},{96,480},{112... | collective-permute-start | bytes 86024 | tf_op jit(solution)/shard_map/ppermute | solution.py:234
  37.1 5.6 %collective-permute-done.got_ref = bf16[16,896]{1,0:T(8,128)(2,1)S(1)} collective-permute-done((bf16[16,896]{1,0:T(8,128)(2,1)S(1)}, bf16[16,896]{1,0:T(8,128)(2,1)S(1)}, u32[]{:S(2)}, u32[]{:S(2)}) %collective-permute-start) | collective-permute-done | bytes 28704 | tf_op jit(solution)/shard_map/ppermute | solution.py:234
  42.8 1.2 %outer_step.1 = (bf16[24,16,896]{2,1,0:T(8,128)(2,1)S(1)}, f32[2,4,896]{2,1,0:T(4,128)}) custom-call(s32[3]{0:T(128)S(1)} %pad_add_fusion.place_ref, bf16[16,896]{1,0:T(8,128)(2,1)S(1)} %get-tuple-element.13.kept_ref, bf16[16,896]{1,0:T(8,128)(2,1)S(1)} %collective-permute-done.got_ref, f32[2,4,896]{2,1,0:T(4,128)S(1)} %copy-done.1, ...), custom_call_target="tpu_custom_call" | custom-call | tf_op jit(solution)/shard_map/outer_step/pallas_call | solution.py:189
  44.0 25.0 %all_to_all.11.got_ref = bf16[24,16,896]{2,1,0:T(8,128)(2,1)S(1)} all-to-all(bf16[24,16,896]{2,1,0:T(8,128)(2,1)S(1)} %get-tuple-element.15), channel_id=1, replica_groups={{128,144,160,176,192,208,224,240,0,16,32,48,64,80,96,112,256,272,288,30..., dimensions={0} | all-to-all | bytes 1376256 | tf_op jit(solution)/shard_map/all_to_all | solution.py:236
  68.9 0.0 copy-done
  68.9 0.0 copy-done.2
  69.0 2.0 %mix.1 = (bf16[2,2,96,896]{3,2,1,0:T(8,128)(2,1)}, f32[2,2,96,896]{3,2,1,0:T(8,128)}) custom-call(s32[2]{0:T(128)S(1)} %copy-done.2, bf16[24,16,896]{2,1,0:T(8,128)(2,1)S(1)} %all_to_all.11.got_ref, bf16[2,2,96,896]{3,2,1,0:T(8,128)(2,1)S(1)} %bitcast.11), custom_call_target="tpu_custom_call" | custom-call | tf_op jit(solution)/shard_map/mix/pallas_call | solution.py:201
Async XLA Ops:
  0.7 33.8 %copy-start.1 = (f32[2,4,896]{2,1,0:T(4,128)S(1)}, f32[2,4,896]{2,1,0:T(4,128)}, u32[]{:S(2)}) copy-start(f32[2,4,896]{2,1,0:T(4,128)} %momentum_ref.3) | copy-start | bytes 86020
  34.5 34.4 %copy-start = (bf16[1,2,192,896]{3,2,1,0:T(8,128)(2,1)S(1)}, bf16[1,2,192,896]{3,2,1,0:T(8,128)(2,1)}, u32[]{:S(2)}) copy-start(bf16[1,2,192,896]{3,2,1,0:T(8,128)(2,1)} %param.5) | copy-start | bytes 2064388
  34.5 34.4 %copy-start.2 = (s32[2]{0:T(128)S(1)}, s32[2]{0:T(128)}, u32[]{:S(2)}) copy-start(s32[2]{0:T(128)} %mix_ref.1) | copy-start | bytes 28
  35.2 7.6 %collective-permute-start = (bf16[16,896]{1,0:T(8,128)(2,1)S(1)}, bf16[16,896]{1,0:T(8,128)(2,1)S(1)}, u32[]{:S(2)}, u32[]{:S(2)}) collective-permute-start(bf16[16,896]{1,0:T(8,128)(2,1)S(1)} %get-tuple-element.13.kept_ref), channel_id=1, source_target_pairs={{0,384},{16,400},{32,416},{48,432},{64,448},{80,464},{96,480},{112... | collective-permute-start | bytes 86024 | tf_op jit(solution)/shard_map/ppermute | solution.py:234

commit v3 on v2

--- a/solution.py
+++ b/solution.py
@@ -19,9 +19,13 @@
 FAR = pl.BlockSpec(memory_space=pltpu.HBM)
 
 
-def slot(member):
-    layer = member // ROUND
-    return (layer ^ 1 if layer < 2 else layer) * ROUND + member % ROUND
+FIRST_IN = (1, 4)
+FIRST_OUT = (1, 0)
+
+
+def slot(member, first):
+    layer, y = member // ROUND - first[0], member % ROUND - first[1]
+    return layer % 3 * ROUND + y % ROUND
 
 
 def low_rows(shape):
@@ -70,7 +74,7 @@
                 pieces[2 * k].append(even[k])
                 pieces[2 * k + 1].append(odd[k])
         for i in range(2 * tiles):
-            out_ref[slot(2 * tiles * step + i)] = jnp.concatenate(pieces[i], axis=0).astype(BF16)
+            out_ref[slot(2 * tiles * step + i, FIRST_IN)] = jnp.concatenate(pieces[i], axis=0).astype(BF16)
     odd = place_ref[1] == 1
     mine = pl.ds(pl.multiple_of(place_ref[2] * 8, 8), 8)
     low = low_rows((8, width))
@@ -104,30 +108,34 @@
     send_ref[...] = jnp.concatenate(sums, axis=0).astype(BF16)
 
 
-def step_kernel(parts, place_ref, kept_ref, got_ref, momentum_ref, own_ref, send_ref, new_ref):
+def step_kernel(place_ref, kept_ref, got_ref, own_ref, send_ref, average_ref):
     mine = place_ref[0]
     total = kept_ref[...].astype(F32) + got_ref[...].astype(F32)
     send = total.astype(BF16)
-    for i in range(parts):
+    for i in range(send_ref.shape[0]):
         send_ref[i] = send
     picked = total[0:8]
     for outer in range(1, OUTER):
         picked = jnp.where(mine == outer, total[8 * outer : 8 * outer + 8], picked)
-    average = (own_ref[...] - picked) * (1.0 / 1.33)
-    for side in range(2):
-        new_ref[side] = 0.9 * momentum_ref[side] + average[4 * side : 4 * side + 4]
-
-
-def mix_kernel(mix_ref, got_ref, local_ref, mixed_hbm, new_hbm, mixed_ref, new_ref, sems):
+    average_ref[...] = (own_ref[...] - picked) * (1.0 / 1.33)
+
+
+def mix_kernel(
+    mix_ref, got_ref, local_ref, momentum_ref, average_ref,
+    mixed_hbm, new_hbm, next_hbm, mixed_ref, new_ref, next_ref, sems,
+):
     _, _, deep, width = new_ref.shape
     tiles = TALL // 8
     top = jnp.full((8, width), mix_ref[0].astype(F32))
     bottom = jnp.full((8, width), mix_ref[1].astype(F32))
     alpha = (top / bottom)[None]
-    stores = []
+    for side in range(2):
+        next_ref[side] = 0.9 * momentum_ref[side] + average_ref[4 * side : 4 * side + 4]
+    stores = [pltpu.make_async_copy(next_ref, next_hbm, sems.at[2 * (deep // TALL)])]
+    stores[0].start()
     for step in range(deep // TALL):
         span = pl.ds(TALL * step, TALL)
-        blocks = [got_ref[slot(2 * tiles * step + i)].astype(F32) for i in range(2 * tiles)]
+        blocks = [got_ref[slot(2 * tiles * step + i, FIRST_OUT)].astype(F32) for i in range(2 * tiles)]
         for outer in range(OUTER):
             rows = slice(8 * outer, 8 * outer + 8)
             even = jnp.stack([blocks[2 * k][rows] for k in range(tiles)])
@@ -184,56 +192,61 @@
     )(place, got, rows, momentum)
 
 
-def outer_step(parts, place, kept, got, momentum, own):
+def outer_step(parts, place, kept, got, own):
     tall, width = got.shape
     return pl.pallas_call(
-        functools.partial(step_kernel, parts),
+        step_kernel,
+        in_specs=[SCALAR, WHOLE, WHOLE, WHOLE],
+        out_specs=[WHOLE, WHOLE],
+        out_shape=[jax.ShapeDtypeStruct((parts, tall, width), BF16), jax.ShapeDtypeStruct(own.shape, F32)],
+        compiler_params=SMALL,
+        name="outer_step",
+    )(place, kept, got, own)
+
+
+def mix(mix_ratio, got, local, momentum, average):
+    deep = local.shape[2]
+    return pl.pallas_call(
+        mix_kernel,
         in_specs=[SCALAR, WHOLE, WHOLE, WHOLE, WHOLE],
-        out_specs=[WHOLE, WHOLE],
-        out_shape=[jax.ShapeDtypeStruct((parts, tall, width), BF16), jax.ShapeDtypeStruct(momentum.shape, F32)],
-        compiler_params=SMALL,
-        name="outer_step",
-    )(place, kept, got, momentum, own)
-
-
-def mix(mix_ratio, got, local):
-    deep = local.shape[2]
-    return pl.pallas_call(
-        mix_kernel,
-        in_specs=[SCALAR, WHOLE, WHOLE],
-        out_specs=[FAR, FAR],
-        out_shape=[jax.ShapeDtypeStruct(local.shape, BF16), jax.ShapeDtypeStruct(local.shape, F32)],
+        out_specs=[FAR, FAR, FAR],
+        out_shape=[
+            jax.ShapeDtypeStruct(local.shape, BF16),
+            jax.ShapeDtypeStruct(local.shape, F32),
+            jax.ShapeDtypeStruct(momentum.shape, F32),
+        ],
         scratch_shapes=[
             pltpu.VMEM(local.shape, BF16),
             pltpu.VMEM(local.shape, F32),
-            pltpu.SemaphoreType.DMA((2 * (deep // TALL),)),
+            pltpu.VMEM(momentum.shape, F32),
+            pltpu.SemaphoreType.DMA((2 * (deep // TALL) + 1,)),
         ],
         compiler_params=SMALL,
         name="mix",
-    )(mix_ratio, got, local)
+    )(mix_ratio, got, local, momentum, average)
 
 
 def shards(local_weights, base_weights, momentum, exponents, mix_ratio):
     replicas = lax.axis_size("rep")
     rows, width = base_weights.shape[1:]
     parts = replicas // OUTER
-    members = sorted(range(parts), key=slot)
-    near = [[o * parts + j for j in members] for o in range(OUTER)]
+    near_in, near_out = (
+        [[o * parts + j for j in sorted(range(parts), key=lambda j: slot(j, first))] for o in range(OUTER)]
+        for first in (FIRST_IN, FIRST_OUT)
+    )
     across = [(r, (r + parts) % replicas) for r in range(replicas)]
     index = lax.axis_index("rep")
     member = lax.rem(index, parts)
     place = jnp.stack([lax.div(index, parts), lax.rem(member, 2), lax.div(member, 2)]).astype(jnp.int32)
-    swap = functools.partial(
-        lax.all_to_all, axis_name="rep", split_axis=0, concat_axis=0, axis_index_groups=near, tiled=True
-    )
+    swap = functools.partial(lax.all_to_all, axis_name="rep", split_axis=0, concat_axis=0, tiled=True)
 
     local = local_weights.reshape(2, OUTER, rows // OUTER, width)
     base = base_weights.reshape(2, OUTER, rows // OUTER, width)
     coded, own_rows = encode(place, jnp.transpose(exponents[0], (2, 0, 1)), local, base)
-    sent, own = partial(replicas, place, swap(coded), own_rows, momentum)
+    sent, own = partial(replicas, place, swap(coded, axis_index_groups=near_in), own_rows, momentum)
     got = lax.ppermute(sent, "rep", across)
-    sent, new_momentum = outer_step(parts, place, sent, got, momentum, own)
-    mixed, new_base = mix(mix_ratio, swap(sent), local)
+    sent, average = outer_step(parts, place, sent, got, own)
+    mixed, new_base, new_momentum = mix(mix_ratio, swap(sent, axis_index_groups=near_out), local, momentum, average)
     return mixed.reshape(local_weights.shape), new_base.reshape(base_weights.shape), new_momentum
 
 

time: 71.2 us -> 67.9 us (0.954)
  the two profiles are of different devices: /device:TPU:198 before, /device:TPU:21 now
where the time goes in v3:
time: 67.9 us; the launch traced here: 67.6 us
  blocking collectives  51.1 us (75%)
  starting transfers between devices  8.83 us (13%)
  Pallas kernels  5.63 us (8%)
  waiting for transfers between devices  1.26 us (2%)
  between operations  0.7 us (1%)
    all_to_all x1, blocking collectives, shards(): swap(coded, axis_index_groups=near_in)  26.1 us
    all_to_all x1, blocking collectives, shards(): swap(sent, axis_index_groups=near_out)  25 us
    ppermute x1, starting transfers between devices, shards(): got = lax.ppermute(sent, 'rep', across)  8.83 us
    pallas_call x1, Pallas kernels, encode(): pl.pallas_call(encode_kernel, in_specs=[SCALAR, FAR, FAR, FAR], out_specs...  2.37 us
    pallas_call x1, Pallas kernels, mix(): pl.pallas_call(mix_kernel, in_specs=[SCALAR, WHOLE, WHOLE, WHOLE, WHOLE],...  2.01 us
  transfers between devices with their start and end apart: 1, of which 1 were waited for; matrix products, arithmetic and copies ran while one was open for 0% of the time, Pallas kernels for 0%

profile of v3, /device:TPU:21, one launch (start us, length us, event | category | flops | bytes accessed | tf_op | source)
XLA Modules:
  0.0 67.6 jit_solution(10687427610923904014)
XLA Ops:
  0.7 0.1 pad_add_fusion.place_ref
  0.7 0.0 copy-start.1
  0.7 2.4 %encode.1 = (bf16[24,16,896]{2,1,0:T(8,128)(2,1)S(1)}, f32[16,896]{1,0:T(8,128)S(1)}) custom-call(s32[3]{0:T(128)S(1)} %pad_add_fusion.place_ref, s32[7,2,192]{2,1,0:T(2,128)} %bitcast.13, bf16[2,2,96,896]{3,2,1,0:T(8,128)(2,1)} %bitcast.10, f32[2,2,96,896]{3,2,1,0:T(8,128)} %bitcast.12), custom_call_target="tpu_custom_call" | custom-call | tf_op jit(solution)/shard_map/encode/pallas_call | solution.py:162
  3.1 26.1 %all_to_all.10.got_ref = bf16[24,16,896]{2,1,0:T(8,128)(2,1)S(1)} all-to-all(bf16[24,16,896]{2,1,0:T(8,128)(2,1)S(1)} %get-tuple-element.12), channel_id=1, replica_groups={{192,208,224,240,128,144,160,176,320,336,352,368,256,272,288,304,64,80,..., dimensions={0} | all-to-all | bytes 1376256 | tf_op jit(solution)/shard_map/all_to_all | solution.py:246
  29.2 0.0 copy-start
  29.2 0.0 copy-start.2
  29.2 0.0 copy-done.1
  29.2 0.7 partial.1
  29.9 8.8 %collective-permute-start = (bf16[16,896]{1,0:T(8,128)(2,1)S(1)}, bf16[16,896]{1,0:T(8,128)(2,1)S(1)}, u32[]{:S(2)}, u32[]{:S(2)}) collective-permute-start(bf16[16,896]{1,0:T(8,128)(2,1)S(1)} %get-tuple-element.14.kept_ref), channel_id=1, source_target_pairs={{0,384},{16,400},{32,416},{48,432},{64,448},{80,464},{96,480},{112... | collective-permute-start | bytes 86024 | tf_op jit(solution)/shard_map/ppermute | solution.py:247
  38.7 1.3 %collective-permute-done.got_ref = bf16[16,896]{1,0:T(8,128)(2,1)S(1)} collective-permute-done((bf16[16,896]{1,0:T(8,128)(2,1)S(1)}, bf16[16,896]{1,0:T(8,128)(2,1)S(1)}, u32[]{:S(2)}, u32[]{:S(2)}) %collective-permute-start) | collective-permute-done | bytes 28704 | tf_op jit(solution)/shard_map/ppermute | solution.py:247
  40.0 0.6 outer_step.1
  40.6 25.0 %all_to_all.11.got_ref = bf16[24,16,896]{2,1,0:T(8,128)(2,1)S(1)} all-to-all(bf16[24,16,896]{2,1,0:T(8,128)(2,1)S(1)} %get-tuple-element.16), channel_id=1, replica_groups={{128,144,160,176,192,208,224,240,256,272,288,304,320,336,352,368,0,16,3..., dimensions={0} | all-to-all | bytes 1376256 | tf_op jit(solution)/shard_map/all_to_all | solution.py:249
  65.6 0.0 copy-done
  65.6 0.0 copy-done.2
  65.6 2.0 %mix.1 = (bf16[2,2,96,896]{3,2,1,0:T(8,128)(2,1)}, f32[2,2,96,896]{3,2,1,0:T(8,128)}, f32[2,4,896]{2,1,0:T(4,128)}) custom-call(s32[2]{0:T(128)S(1)} %copy-done.2, bf16[24,16,896]{2,1,0:T(8,128)(2,1)S(1)} %all_to_all.11.got_ref, bf16[2,2,96,896]{3,2,1,0:T(8,128)(2,1)S(1)} %bitcast.11, f32[2,4,896]{2,1,0:T(4,128)S(1)} %copy-done.1, ...), custom_call_target="tpu_custom_call" | custom-call | tf_op jit(solution)/shard_map/mix/pallas_call | solution.py:209
Async XLA Ops:
  0.7 28.5 %copy-start.1 = (f32[2,4,896]{2,1,0:T(4,128)S(1)}, f32[2,4,896]{2,1,0:T(4,128)}, u32[]{:S(2)}) copy-start(f32[2,4,896]{2,1,0:T(4,128)} %momentum_ref.3) | copy-start | bytes 86020
  29.2 36.4 %copy-start = (bf16[1,2,192,896]{3,2,1,0:T(8,128)(2,1)S(1)}, bf16[1,2,192,896]{3,2,1,0:T(8,128)(2,1)}, u32[]{:S(2)}) copy-start(bf16[1,2,192,896]{3,2,1,0:T(8,128)(2,1)} %param.5) | copy-start | bytes 2064388
  29.2 36.4 %copy-start.2 = (s32[2]{0:T(128)S(1)}, s32[2]{0:T(128)}, u32[]{:S(2)}) copy-start(s32[2]{0:T(128)} %mix_ref.1) | copy-start | bytes 28
  29.9 10.1 %collective-permute-start = (bf16[16,896]{1,0:T(8,128)(2,1)S(1)}, bf16[16,896]{1,0:T(8,128)(2,1)S(1)}, u32[]{:S(2)}, u32[]{:S(2)}) collective-permute-start(bf16[16,896]{1,0:T(8,128)(2,1)S(1)} %get-tuple-element.14.kept_ref), channel_id=1, source_target_pairs={{0,384},{16,400},{32,416},{48,432},{64,448},{80,464},{96,480},{112... | collective-permute-start | bytes 86024 | tf_op jit(solution)/shard_map/ppermute | solution.py:247

commit v4 on v3

--- a/solution.py
+++ b/solution.py
@@ -10,7 +10,7 @@
 BLOCK = 128
 OUTER = 2
 ROUND = 8
-TALL = 16
+TALL = 32
 F32 = jnp.float32
 BF16 = jnp.bfloat16
 SMALL = pltpu.CompilerParams(vmem_limit_bytes=12 << 20)
@@ -20,7 +20,7 @@
 
 
 FIRST_IN = (1, 4)
-FIRST_OUT = (1, 0)
+FIRST_OUT = (2, 0)
 
 
 def slot(member, first):

time: 67.9 us -> 68.7 us (1.012)
  the two profiles are of different devices: /device:TPU:21 before, /device:TPU:14 now
where the time goes in v4:
time: 68.7 us; the launch traced here: 68.5 us
  blocking collectives  50.5 us (74%)
  starting transfers between devices  9.41 us (14%)
  Pallas kernels  5.58 us (8%)
  waiting for transfers between devices  2.14 us (3%)
  between operations  0.7 us (1%)
    all_to_all x1, blocking collectives, shards(): swap(coded, axis_index_groups=near_in)  27.3 us
    all_to_all x1, blocking collectives, shards(): swap(sent, axis_index_groups=near_out)  23.2 us
    ppermute x1, starting transfers between devices, shards(): got = lax.ppermute(sent, 'rep', across)  9.41 us
    pallas_call x1, Pallas kernels, encode(): pl.pallas_call(encode_kernel, in_specs=[SCALAR, FAR, FAR, FAR], out_specs...  2.3 us
    ppermute x1, waiting for transfers between devices, shards(): got = lax.ppermute(sent, 'rep', across)  2.14 us
    pallas_call x1, Pallas kernels, mix(): pl.pallas_call(mix_kernel, in_specs=[SCALAR, WHOLE, WHOLE, WHOLE, WHOLE],...  2.03 us
  transfers between devices with their start and end apart: 1, of which 1 were waited for; matrix products, arithmetic and copies ran while one was open for 0% of the time, Pallas kernels for 0%

profile of v4, /device:TPU:14, one launch (start us, length us, event | category | flops | bytes accessed | tf_op | source)
XLA Modules:
  0.0 68.5 jit_solution(10927624747050544690)
XLA Ops:
  0.7 0.1 pad_add_fusion.place_ref
  0.7 0.0 copy-start.1
  0.7 2.3 %encode.1 = (bf16[24,16,896]{2,1,0:T(8,128)(2,1)S(1)}, f32[16,896]{1,0:T(8,128)S(1)}) custom-call(s32[3]{0:T(128)S(1)} %pad_add_fusion.place_ref, s32[7,2,192]{2,1,0:T(2,128)} %bitcast.13, bf16[2,2,96,896]{3,2,1,0:T(8,128)(2,1)} %bitcast.10, f32[2,2,96,896]{3,2,1,0:T(8,128)} %bitcast.12), custom_call_target="tpu_custom_call" | custom-call | tf_op jit(solution)/shard_map/encode/pallas_call | solution.py:162
  3.0 27.3 %all_to_all.10.got_ref = bf16[24,16,896]{2,1,0:T(8,128)(2,1)S(1)} all-to-all(bf16[24,16,896]{2,1,0:T(8,128)(2,1)S(1)} %get-tuple-element.12), channel_id=1, replica_groups={{192,208,224,240,128,144,160,176,320,336,352,368,256,272,288,304,64,80,..., dimensions={0} | all-to-all | bytes 1376256 | tf_op jit(solution)/shard_map/all_to_all | solution.py:246
  30.4 0.0 copy-start
  30.4 0.0 copy-start.2
  30.4 0.0 copy-done.1
  30.4 0.7 partial.1
  31.0 9.4 %collective-permute-start = (bf16[16,896]{1,0:T(8,128)(2,1)S(1)}, bf16[16,896]{1,0:T(8,128)(2,1)S(1)}, u32[]{:S(2)}, u32[]{:S(2)}) collective-permute-start(bf16[16,896]{1,0:T(8,128)(2,1)S(1)} %get-tuple-element.14.kept_ref), channel_id=1, source_target_pairs={{0,384},{16,400},{32,416},{48,432},{64,448},{80,464},{96,480},{112... | collective-permute-start | bytes 86024 | tf_op jit(solution)/shard_map/ppermute | solution.py:247
  40.4 2.1 %collective-permute-done.got_ref = bf16[16,896]{1,0:T(8,128)(2,1)S(1)} collective-permute-done((bf16[16,896]{1,0:T(8,128)(2,1)S(1)}, bf16[16,896]{1,0:T(8,128)(2,1)S(1)}, u32[]{:S(2)}, u32[]{:S(2)}) %collective-permute-start) | collective-permute-done | bytes 28704 | tf_op jit(solution)/shard_map/ppermute | solution.py:247
  42.6 0.6 outer_step.1
  43.2 23.2 %all_to_all.11.got_ref = bf16[24,16,896]{2,1,0:T(8,128)(2,1)S(1)} all-to-all(bf16[24,16,896]{2,1,0:T(8,128)(2,1)S(1)} %get-tuple-element.16), channel_id=1, replica_groups={{256,272,288,304,320,336,352,368,0,16,32,48,64,80,96,112,128,144,160,17..., dimensions={0} | all-to-all | bytes 1376256 | tf_op jit(solution)/shard_map/all_to_all | solution.py:249
  66.4 0.0 copy-done
  66.4 0.0 copy-done.2
  66.4 2.0 %mix.1 = (bf16[2,2,96,896]{3,2,1,0:T(8,128)(2,1)}, f32[2,2,96,896]{3,2,1,0:T(8,128)}, f32[2,4,896]{2,1,0:T(4,128)}) custom-call(s32[2]{0:T(128)S(1)} %copy-done.2, bf16[24,16,896]{2,1,0:T(8,128)(2,1)S(1)} %all_to_all.11.got_ref, bf16[2,2,96,896]{3,2,1,0:T(8,128)(2,1)S(1)} %bitcast.11, f32[2,4,896]{2,1,0:T(4,128)S(1)} %copy-done.1, ...), custom_call_target="tpu_custom_call" | custom-call | tf_op jit(solution)/shard_map/mix/pallas_call | solution.py:209
Async XLA Ops:
  0.7 29.6 %copy-start.1 = (f32[2,4,896]{2,1,0:T(4,128)S(1)}, f32[2,4,896]{2,1,0:T(4,128)}, u32[]{:S(2)}) copy-start(f32[2,4,896]{2,1,0:T(4,128)} %momentum_ref.3) | copy-start | bytes 86020
  30.4 36.1 %copy-start = (bf16[1,2,192,896]{3,2,1,0:T(8,128)(2,1)S(1)}, bf16[1,2,192,896]{3,2,1,0:T(8,128)(2,1)}, u32[]{:S(2)}) copy-start(bf16[1,2,192,896]{3,2,1,0:T(8,128)(2,1)} %param.5) | copy-start | bytes 2064388
  30.4 36.1 %copy-start.2 = (s32[2]{0:T(128)S(1)}, s32[2]{0:T(128)}, u32[]{:S(2)}) copy-start(s32[2]{0:T(128)} %mix_ref.1) | copy-start | bytes 28
  31.0 11.6 %collective-permute-start = (bf16[16,896]{1,0:T(8,128)(2,1)S(1)}, bf16[16,896]{1,0:T(8,128)(2,1)S(1)}, u32[]{:S(2)}, u32[]{:S(2)}) collective-permute-start(bf16[16,896]{1,0:T(8,128)(2,1)S(1)} %get-tuple-element.14.kept_ref), channel_id=1, source_target_pairs={{0,384},{16,400},{32,416},{48,432},{64,448},{80,464},{96,480},{112... | collective-permute-start | bytes 86024 | tf_op jit(solution)/shard_map/ppermute | solution.py:247

commit v5 on v3

--- a/solution.py
+++ b/solution.py
@@ -19,8 +19,8 @@
 FAR = pl.BlockSpec(memory_space=pltpu.HBM)
 
 
-FIRST_IN = (1, 4)
-FIRST_OUT = (1, 0)
+FIRST_IN = (2, 4)
+FIRST_OUT = (0, 0)
 
 
 def slot(member, first):

time: 67.9 us -> 69.3 us (1.021)
  the two profiles are of different devices: /device:TPU:21 before, /device:TPU:14 now
where the time goes in v5:
time: 69.3 us; the launch traced here: 69.1 us
  blocking collectives  51.4 us (74%)
  starting transfers between devices  9.14 us (13%)
  Pallas kernels  5.63 us (8%)
  waiting for transfers between devices  2.14 us (3%)
  between operations  0.7 us (1%)
    all_to_all x1, blocking collectives, shards(): swap(coded, axis_index_groups=near_in)  28.5 us
    all_to_all x1, blocking collectives, shards(): swap(sent, axis_index_groups=near_out)  22.9 us
    ppermute x1, starting transfers between devices, shards(): got = lax.ppermute(sent, 'rep', across)  9.14 us
    pallas_call x1, Pallas kernels, encode(): pl.pallas_call(encode_kernel, in_specs=[SCALAR, FAR, FAR, FAR], out_specs...  2.37 us
    ppermute x1, waiting for transfers between devices, shards(): got = lax.ppermute(sent, 'rep', across)  2.14 us
    pallas_call x1, Pallas kernels, mix(): pl.pallas_call(mix_kernel, in_specs=[SCALAR, WHOLE, WHOLE, WHOLE, WHOLE],...  2.01 us
  transfers between devices with their start and end apart: 1, of which 1 were waited for; matrix products, arithmetic and copies ran while one was open for 0% of the time, Pallas kernels for 0%

profile of v5, /device:TPU:14, one launch (start us, length us, event | category | flops | bytes accessed | tf_op | source)
XLA Modules:
  0.0 69.1 jit_solution(14960381892605905646)
XLA Ops:
  0.7 0.1 pad_add_fusion.place_ref
  0.7 0.0 copy-start.1
  0.7 2.4 %encode.1 = (bf16[24,16,896]{2,1,0:T(8,128)(2,1)S(1)}, f32[16,896]{1,0:T(8,128)S(1)}) custom-call(s32[3]{0:T(128)S(1)} %pad_add_fusion.place_ref, s32[7,2,192]{2,1,0:T(2,128)} %bitcast.13, bf16[2,2,96,896]{3,2,1,0:T(8,128)(2,1)} %bitcast.10, f32[2,2,96,896]{3,2,1,0:T(8,128)} %bitcast.12), custom_call_target="tpu_custom_call" | custom-call | tf_op jit(solution)/shard_map/encode/pallas_call | solution.py:162
  3.1 28.5 %all_to_all.10.got_ref = bf16[24,16,896]{2,1,0:T(8,128)(2,1)S(1)} all-to-all(bf16[24,16,896]{2,1,0:T(8,128)(2,1)S(1)} %get-tuple-element.12), channel_id=1, replica_groups={{320,336,352,368,256,272,288,304,64,80,96,112,0,16,32,48,192,208,224,24..., dimensions={0} | all-to-all | bytes 1376256 | tf_op jit(solution)/shard_map/all_to_all | solution.py:246
  31.6 0.0 copy-start
  31.6 0.0 copy-start.2
  31.6 0.0 copy-done.1
  31.6 0.7 partial.1
  32.2 9.1 %collective-permute-start = (bf16[16,896]{1,0:T(8,128)(2,1)S(1)}, bf16[16,896]{1,0:T(8,128)(2,1)S(1)}, u32[]{:S(2)}, u32[]{:S(2)}) collective-permute-start(bf16[16,896]{1,0:T(8,128)(2,1)S(1)} %get-tuple-element.14.kept_ref), channel_id=1, source_target_pairs={{0,384},{16,400},{32,416},{48,432},{64,448},{80,464},{96,480},{112... | collective-permute-start | bytes 86024 | tf_op jit(solution)/shard_map/ppermute | solution.py:247
  41.4 2.1 %collective-permute-done.got_ref = bf16[16,896]{1,0:T(8,128)(2,1)S(1)} collective-permute-done((bf16[16,896]{1,0:T(8,128)(2,1)S(1)}, bf16[16,896]{1,0:T(8,128)(2,1)S(1)}, u32[]{:S(2)}, u32[]{:S(2)}) %collective-permute-start) | collective-permute-done | bytes 28704 | tf_op jit(solution)/shard_map/ppermute | solution.py:247
  43.5 0.6 outer_step.1
  44.1 22.9 %all_to_all.11.got_ref = bf16[24,16,896]{2,1,0:T(8,128)(2,1)S(1)} all-to-all(bf16[24,16,896]{2,1,0:T(8,128)(2,1)S(1)} %get-tuple-element.16), channel_id=1, replica_groups={{0,16,32,48,64,80,96,112,128,144,160,176,192,208,224,240,256,272,288,30..., dimensions={0} | all-to-all | bytes 1376256 | tf_op jit(solution)/shard_map/all_to_all | solution.py:249
  67.1 0.0 copy-done
  67.1 0.0 copy-done.2
  67.1 2.0 %mix.1 = (bf16[2,2,96,896]{3,2,1,0:T(8,128)(2,1)}, f32[2,2,96,896]{3,2,1,0:T(8,128)}, f32[2,4,896]{2,1,0:T(4,128)}) custom-call(s32[2]{0:T(128)S(1)} %copy-done.2, bf16[24,16,896]{2,1,0:T(8,128)(2,1)S(1)} %all_to_all.11.got_ref, bf16[2,2,96,896]{3,2,1,0:T(8,128)(2,1)S(1)} %bitcast.11, f32[2,4,896]{2,1,0:T(4,128)S(1)} %copy-done.1, ...), custom_call_target="tpu_custom_call" | custom-call | tf_op jit(solution)/shard_map/mix/pallas_call | solution.py:209
Async XLA Ops:
  0.7 30.8 %copy-start.1 = (f32[2,4,896]{2,1,0:T(4,128)S(1)}, f32[2,4,896]{2,1,0:T(4,128)}, u32[]{:S(2)}) copy-start(f32[2,4,896]{2,1,0:T(4,128)} %momentum_ref.3) | copy-start | bytes 86020
  31.6 35.5 %copy-start = (bf16[1,2,192,896]{3,2,1,0:T(8,128)(2,1)S(1)}, bf16[1,2,192,896]{3,2,1,0:T(8,128)(2,1)}, u32[]{:S(2)}) copy-start(bf16[1,2,192,896]{3,2,1,0:T(8,128)(2,1)} %param.5) | copy-start | bytes 2064388
  31.6 35.5 %copy-start.2 = (s32[2]{0:T(128)S(1)}, s32[2]{0:T(128)}, u32[]{:S(2)}) copy-start(s32[2]{0:T(128)} %mix_ref.1) | copy-start | bytes 28
  32.2 11.3 %collective-permute-start = (bf16[16,896]{1,0:T(8,128)(2,1)S(1)}, bf16[16,896]{1,0:T(8,128)(2,1)S(1)}, u32[]{:S(2)}, u32[]{:S(2)}) collective-permute-start(bf16[16,896]{1,0:T(8,128)(2,1)S(1)} %get-tuple-element.14.kept_ref), channel_id=1, source_target_pairs={{0,384},{16,400},{32,416},{48,432},{64,448},{80,464},{96,480},{112... | collective-permute-start | bytes 86024 | tf_op jit(solution)/shard_map/ppermute | solution.py:247
